TPU v7x, 512 devices: a whole 4x4x16 slice. The times are simulated.
512 devices in a mesh: batch: 4 (over y), tm: 16 (over x, z_lo), space: 8 (over z_hi, core).
Axes of the slice: x: 4, y: 4, z: 16 (z_hi: 4, z_lo: 4; z = z_hi * 4 + z_lo), core: 2. Of those that a mesh axis runs over, the one named last changes fastest.
Arguments:
- tokens: bfloat16 [64, 1024, 1152], P(('batch', 'tm'), 'space'), parts along dimension 0, may hold values from -6 to 6
- frame_qkv: bfloat16 [1152, 3456], P(None, 'space'), may hold values from -4 to 4
- frame_out: bfloat16 [1152, 1152], P('space'), may hold values from -0.375 to 0.375
- time_qkv: bfloat16 [3456, 1152], P('tm'), may hold values from -4 to 4
- time_out: bfloat16 [1152, 1152], replicated, may hold values from -0.375 to 0.375
- modulation: float32 [8, 3, 1152], P('batch'), parts along dimension 0, may hold values from -4 to 4
Outputs:
- blended: bfloat16 [64, 1024, 1152], P(('batch', 'tm'), 'space'), parts along dimension 0
There are 4 independent parts, one for each index of `batch`. A program takes and returns all parts, laid end to end along the dimension named above; an argument that names none is the same for every part. Nothing has to cross between parts.
All inputs are finite; a program needn't handle non-finite values.
Results may differ from a plain program's by a relative error of at most 0.035.
Values may be sent and summed in bfloat16 or wider, within the bound.
No kernel may reach another device: no remote copies, remote signals or barrier semaphores. Data moves between devices by JAX's collectives and lax.ppermute only.
A program may use at most 64 MiB of HBM per device.

v0:
```python
import jax
import jax.numpy as jnp
from jax import lax
from jax.sharding import PartitionSpec as P

HD = 72
eps_norm = 1e-06


def modulate(tokens, offset, stretch):
    values = tokens.astype(jnp.float32)
    center = jnp.mean(values, axis=-1, keepdims=True)
    spread = jnp.mean(jnp.square(values - center), axis=-1, keepdims=True)
    normed = (values - center) * lax.rsqrt(spread + eps_norm)
    return (normed * (1.0 + stretch) + offset).astype(jnp.bfloat16)


def normalized_weights(scores):
    largest = jnp.max(scores, axis=-1, keepdims=True)
    raised = jnp.exp(scores - largest)
    return (raised / jnp.sum(raised, axis=-1, keepdims=True)).astype(jnp.bfloat16)


def frame_block(queries, key_part, value_part, factor):
    scores = (
        jnp.einsum("fqhe,fkhe->fhqk", queries, key_part, preferred_element_type=jnp.float32)
        * factor
    )
    weights = normalized_weights(scores)
    return jnp.einsum(
        "fhqk,fkhe->fqhe", weights, value_part, preferred_element_type=jnp.float32
    ).astype(jnp.bfloat16)


def frame_attention(triples, head_width):
    frames, spatial, head_count = (triples.shape[0], triples.shape[1], triples.shape[2])
    queries = triples[:, :, :, 0]
    key_part = triples[:, :, :, 1]
    value_part = triples[:, :, :, 2]
    block_rows = min(spatial, 512)
    block_count = spatial // block_rows
    grouped = jnp.moveaxis(
        queries.reshape(frames, block_count, block_rows, head_count, head_width), 1, 0
    )
    results = lax.map(
        lambda query_block: frame_block(query_block, key_part, value_part, head_width ** (-0.5)),
        grouped,
    )
    return jnp.moveaxis(results, 0, 1).reshape(frames, spatial, head_count * head_width)


def time_attention(triples, head_width):
    queries = triples[..., :head_width]
    key_part = triples[..., head_width : 2 * head_width]
    value_part = triples[..., 2 * head_width :]
    scores = jnp.einsum(
        "tshe,ushe->shtu", queries, key_part, preferred_element_type=jnp.float32
    ) * head_width ** (-0.5)
    weights = normalized_weights(scores)
    return jnp.einsum(
        "shtu,ushe->tshe", weights, value_part, preferred_element_type=jnp.float32
    ).astype(jnp.bfloat16)


def shards(tokens, frame_qkv, frame_out, time_qkv, time_out, modulation):
    frames, row_count, model_width = tokens.shape
    first_input = modulate(tokens, modulation[0, 0], modulation[0, 1])
    triples = jnp.einsum(
        "fsd,dc->fsc",
        lax.all_gather(first_input, "space", axis=1, tiled=True),
        frame_qkv,
        preferred_element_type=jnp.float32,
    ).astype(jnp.bfloat16)
    local_heads = frame_qkv.shape[1] // (3 * HD)
    triples = triples.reshape(frames, triples.shape[1], local_heads, 3, HD)
    attended = frame_attention(triples, HD)
    frame_source = attended.reshape(-1, attended.shape[2])
    frame_branch = lax.psum_scatter(
        jnp.dot(frame_source, frame_out, preferred_element_type=jnp.float32).astype(jnp.bfloat16),
        "space",
        scatter_dimension=0,
        tiled=True,
    ).astype(jnp.float32)
    frame_branch = frame_branch.reshape(frames, row_count, model_width)
    middle = (tokens.astype(jnp.float32) + modulation[0, 2] * frame_branch).astype(jnp.bfloat16)
    second_input = modulate(middle, modulation[1, 0], modulation[1, 1])
    second_flat = second_input.reshape(frames * row_count, model_width)
    projected = lax.dot_general(
        second_flat,
        lax.all_gather(time_qkv, "tm", axis=0, tiled=True),
        (((1,), (1,)), ((), ())),
        preferred_element_type=jnp.float32,
    ).astype(jnp.bfloat16)
    head_total = projected.shape[1] // (3 * HD)
    projected = projected.reshape(frames, row_count, head_total, 3 * HD)
    attended = time_attention(
        lax.all_to_all(projected, "tm", split_axis=2, concat_axis=0, tiled=True), HD
    )
    total_frames = attended.shape[0]
    attended = attended.reshape(total_frames, row_count, -1)
    returned = lax.all_to_all(attended, "tm", split_axis=0, concat_axis=2, tiled=True)
    time_branch = jnp.dot(
        returned.reshape(frames * row_count, model_width),
        time_out,
        preferred_element_type=jnp.float32,
    )
    time_branch = time_branch.reshape(frames, row_count, model_width)
    return (middle.astype(jnp.float32) + modulation[1, 2] * time_branch).astype(jnp.bfloat16)


def solution(mesh):
    placed = (
        P(("batch", "tm"), "space", None),
        P(None, "space"),
        P("space", None),
        P("tm", None),
        P(),
        P("batch", None, None),
    )
    return jax.shard_map(
        shards,
        mesh=mesh,
        in_specs=placed,
        out_specs=P(("batch", "tm"), "space", None),
        check_vma=False,
    )
```

profile of v0, /device:TPU:264, one launch (start us, length us, event | category | flops | bytes accessed | tf_op | source)
XLA Modules:
  0.0 395.8 jit_solution(1781436888458273317)
XLA Ops:
  8.4 1.1 convert_reduce_fusion.1
  9.5 1.2 fusion.52
  10.7 1.9 fusion.55
  12.7 60.6 %all-gather.3.cloned.1.call-done = bf16[1,1024,1152]{2,1,0:T(8,128)(2,1)} async-done(((bf16[1,128,1152]{2,1,0:T(8,128)(2,1)}), bf16[1,1024,1152]{2,1,0:T(8,128)(2,1)}) %all-gather.3.cloned.1.call-update) | async-done | bytes 2359312 | tf_op jit(solution)/shard_map/all_gather | solution.py:70
  73.3 3.2 fusion.39
  78.4 16.3 %while.10 = (s32[]{:T(128)}, bf16[2,1,512,2,72]{2,4,3,1,0:T(8,128)(2,1)}, bf16[2,1,512,2,72]{2,4,3,1,0:T(8,128)(2,1)}, bf16[1,1024,2,72]{1,3,2,0:T(8,128)(2,1)}, bf16[1,1024,2,72]{1,3,2,0:T(8,128)(2,1)}, /*index=5*/s32[]{:T(128)}) while((s32[]{:T(128)}, bf16[2,1,512,2,72]{2,4,3,1,0:T(8,128)(2,1)}, bf16[2,1,512,2,72]{2,4,3,1,0:T(8,128)(2,1)}, ...), condition=%wide.region_5.6_spmd, body=%wide.region_2.5_spmd.sunk | while | flops 307307520 | bytes 10462305 | solution.py:45
  78.4 4.5 %fusion.91 = (f32[2,512]{1,0:T(2,128)S(1)}, f32[2,512,1024]{2,1,0:T(8,128)}) fusion(bf16[1,1024,2,72]{1,3,2,0:T(8,128)(2,1)} %get-tuple-element.118, bf16[2,1,512,2,72]{2,4,3,1,0:T(8,128)(2,1)} %get-tuple-element.117, s32[]{:T(128)} %get-tuple-element.109), kind=kOutput, calls=%fused_computation.80.clone.1 | convolution fusion | flops 154141696 | bytes 4641280 | tf_op jit(solution)/shard_map/while/body/eval_jaxpr/sub | solution.py:20
  82.9 3.7 fusion.92
  86.6 4.4 %fusion.91 = (f32[2,512]{1,0:T(2,128)S(1)}, f32[2,512,1024]{2,1,0:T(8,128)}) fusion(bf16[1,1024,2,72]{1,3,2,0:T(8,128)(2,1)} %get-tuple-element.118, bf16[2,1,512,2,72]{2,4,3,1,0:T(8,128)(2,1)} %get-tuple-element.117, s32[]{:T(128)} %get-tuple-element.109), kind=kOutput, calls=%fused_computation.80.clone.1 | convolution fusion | flops 154141696 | bytes 4641280 | tf_op jit(solution)/shard_map/while/body/eval_jaxpr/sub | solution.py:20
  91.0 3.7 fusion.92
  94.7 1.3 copy.23
  96.0 2.4 convolution_convert_fusion.1
  99.0 118.0 %reduce-scatter.2.cloned.1.call-done = bf16[128,1152]{1,0:T(8,128)(2,1)} async-done(((bf16[1024,1152]{1,0:T(8,128)(2,1)}), bf16[128,1152]{1,0:T(8,128)(2,1)}) %reduce-scatter.2.cloned.1.call-update) | async-done | bytes 294928 | tf_op jit(solution)/shard_map/reduce_scatter | solution.py:78
  217.0 1.2 convert_reduce_fusion
  218.4 107.8 %all-gather.5.cloned.1.call-done = bf16[3456,1152]{1,0:T(8,128)(2,1)} async-done(((bf16[216,1152]{1,0:T(8,128)(2,1)}), bf16[3456,1152]{1,0:T(8,128)(2,1)}) %all-gather.5.cloned.1.call-update) | async-done | bytes 7962640 | tf_op jit(solution)/shard_map/all_gather | solution.py:90
  326.3 6.8 %convolution_convert_fusion = bf16[128,3456]{1,0:T(8,128)(2,1)} fusion(bf16[3456,1152]{1,0:T(8,128)(2,1)} %all-gather.5.cloned.1.call-done, bf16[1,128,1152]{2,1,0:T(8,128)(2,1)S(1)} %get-tuple-element.60, f32[1152]{0:T(1024)S(1)} %get-tuple-element.47, f32[1152]{0:T(1024)S(1)} %get-tuple-element.48, f32[128]{0:T(128)S(1)} %add_rsqrt_fusion, ...), kind=kOutput, calls=%fused_computation.23 | convolution fusion | flops 1020542976 | bytes 9152512 | tf_op jit(solution)/shard_map/dot_general | solution.py:88
  333.1 2.2 copy.24
  335.3 28.0 %all_to_all.33 = bf16[1,128,16,216]{1,3,0,2:T(8,128)(2,1)} all-to-all(bf16[1,128,16,216]{1,3,0,2:T(8,128)(2,1)} %bitcast.128), channel_id=1, replica_groups=mesh['batch'=4,'tm'=16,'space'=8] {'tm'}, dimensions={2} | all-to-all | bytes 1769472 | tf_op jit(solution)/shard_map/all_to_all | solution.py:97
  363.3 2.7 copy.26
  366.0 3.2 fusion.76
  369.1 2.7 fusion.43
  371.8 1.5 copy.28
  373.2 13.8 %all_to_all.34 = bf16[16,128,72]{1,2,0:T(8,128)(2,1)S(1)} all-to-all(bf16[16,128,72]{1,2,0:T(8,128)(2,1)S(1)} %copy.28), channel_id=1, replica_groups=mesh['batch'=4,'tm'=16,'space'=8] {'tm'}, dimensions={0} | all-to-all | bytes 589824 | tf_op jit(solution)/shard_map/all_to_all | solution.py:101
  387.0 1.3 fusion.35
  (27 shorter events, 3.8 us)
Async XLA Ops:
  7.4 379.7 %copy-start = (bf16[1152,1152]{1,0:T(8,128)(2,1)S(1)}, bf16[1152,1152]{1,0:T(8,128)(2,1)}, u32[]{:S(2)}) copy-start(bf16[1152,1152]{1,0:T(8,128)(2,1)} %param.12) | copy-start | bytes 7962628
  7.4 65.9 %all-gather.3.cloned.1.call-start = ((), (), s32[]{:S(2)}) async-start(), calls=%async_computation.3 | async-start | bytes 2654208 | tf_op jit(solution)/shard_map/all_gather | solution.py:70
  12.6 204.4 %reduce-scatter.2.cloned.1.call-start = ((), (), s32[]{:S(2)}) async-start(), calls=%async_computation.4 | async-start | bytes 2654208 | tf_op jit(solution)/shard_map/reduce_scatter | solution.py:78
  78.4 17.6 %copy-start.2 = (bf16[144,1152]{1,0:T(8,128)(2,1)S(1)}, bf16[144,1152]{1,0:T(8,128)(2,1)}, u32[]{:S(2)}) copy-start(bf16[144,1152]{1,0:T(8,128)(2,1)} %param.10) | copy-start | bytes 995332
  78.4 4.5 %copy-start.3 = (bf16[1,1024,2,72]{1,3,2,0:T(8,128)(2,1)S(1)}, bf16[1,1024,2,72]{1,3,2,0:T(8,128)(2,1)}, u32[]{:S(2)}) copy-start(bf16[1,1024,2,72]{1,3,2,0:T(8,128)(2,1)} %get-tuple-element.119) | copy-start | bytes 884740 | tf_op jit(solution)/shard_map/while
  86.6 4.4 %copy-start.3 = (bf16[1,1024,2,72]{1,3,2,0:T(8,128)(2,1)S(1)}, bf16[1,1024,2,72]{1,3,2,0:T(8,128)(2,1)}, u32[]{:S(2)}) copy-start(bf16[1,1024,2,72]{1,3,2,0:T(8,128)(2,1)} %get-tuple-element.119) | copy-start | bytes 884740 | tf_op jit(solution)/shard_map/while
  94.7 122.4 %copy-start.1 = (bf16[1,128,1152]{2,1,0:T(8,128)(2,1)S(1)}, bf16[1,128,1152]{2,1,0:T(8,128)(2,1)}, u32[]{:S(2)}) copy-start(bf16[1,128,1152]{2,1,0:T(8,128)(2,1)} %param.8) | copy-start | bytes 884740
  98.5 227.8 %all-gather.5.cloned.1.call-start = ((), (), s32[]{:S(2)}) async-start(), calls=%async_computation.5 | async-start | bytes 8460288 | tf_op jit(solution)/shard_map/all_gather | solution.py:90
Sparse Core Ops, SparseCore 0:
  12.8 60.4 all-gather.2
  98.6 118.4 reduce-scatter.1
Sparse Core Ops, SparseCore 1:
  101.0 225.2 all-gather.4
where the time goes:
time: 396 us
  waiting for transfers between devices  287 us (72%)
  blocking collectives  41.8 us (11%)
  matrix products  35.8 us (9%)
  between operations  14.9 us (4%)
  local copies, waits for them, and re-layouts  9.56 us (2%)
  other arithmetic  6.63 us (2%)
    reduce_scatter x1, waiting for transfers between devices, shards(): lax.psum_scatter(jnp.dot(frame_source, frame_out, preferred_element_type=...  118 us
    all_gather x1, waiting for transfers between devices, shards(): lax.all_gather(time_qkv, 'tm', axis=0, tiled=True)  108 us
    all_gather x1, waiting for transfers between devices, shards(): lax.all_gather(first_input, 'space', axis=1, tiled=True)  60.6 us
    all_to_all x1, blocking collectives, shards(): lax.all_to_all(projected, 'tm', split_axis=2, concat_axis=0, tiled=True)  28 us
    all_to_all x1, blocking collectives, shards(): lax.all_to_all(attended, 'tm', split_axis=0, concat_axis=2, tiled=True)  13.8 us
    sub x3, matrix products, normalized_weights(): raised = jnp.exp(scores - largest)  12 us
  transfers between devices with their start and end apart: 3, of which 3 were waited for; matrix products, arithmetic and copies ran while one was open for 0% of the time, Pallas kernels for 0%

commit v1 on v0

--- a/solution.py
+++ b/solution.py
@@ -87,7 +87,9 @@
     second_flat = second_input.reshape(frames * row_count, model_width)
     projected = lax.dot_general(
         second_flat,
-        lax.all_gather(time_qkv, "tm", axis=0, tiled=True),
+        jnp.concatenate(
+            lax.all_to_all(jnp.stack([time_qkv] * lax.axis_size("tm")), "tm", 0, 0), axis=0
+        ),
         (((1,), (1,)), ((), ())),
         preferred_element_type=jnp.float32,
     ).astype(jnp.bfloat16)

time: 396 us -> 366 us (0.924)
  the two profiles are of different devices: /device:TPU:264 before, /device:TPU:1 now
where the time goes in v1:
time: 366 us; the launch traced here: 365 us
  waiting for transfers between devices  246 us (67%)
  blocking collectives  42.5 us (12%)
  matrix products  35.8 us (10%)
  local copies, waits for them, and re-layouts  14.5 us (4%)
  between operations  13.5 us (4%)
  starting transfers between devices  9.27 us (3%)
    reduce_scatter x1, waiting for transfers between devices, shards(): lax.psum_scatter(jnp.dot(frame_source, frame_out, preferred_element_type=...  181 us
    all_gather x1, waiting for transfers between devices, shards(): lax.all_gather(first_input, 'space', axis=1, tiled=True)  64.6 us
    all_to_all x1, blocking collectives, shards(): lax.all_to_all(projected, 'tm', split_axis=2, concat_axis=0, tiled=True)  28.9 us
    all_to_all x1, blocking collectives, shards(): lax.all_to_all(attended, 'tm', split_axis=0, concat_axis=2, tiled=True)  13.6 us
    sub x3, matrix products, normalized_weights(): raised = jnp.exp(scores - largest)  12 us
    all_to_all x1, starting transfers between devices, shards(): lax.all_to_all(jnp.stack([time_qkv] * lax.axis_size('tm')), 'tm', 0, 0)  9.19 us
    dot_general x2, matrix products, frame_block(): jnp.einsum('fhqk,fkhe->fqhe', weights, value_part, preferred_element_type...  7.44 us
  transfers between devices with their start and end apart: 3, of which 2 were waited for; matrix products, arithmetic and copies ran while one was open for 8% of the time, Pallas kernels for 0%

profile of v1, /device:TPU:1, one launch (start us, length us, event | category | flops | bytes accessed | tf_op | source)
XLA Modules:
  0.0 364.9 jit_solution(8733172773233728273)
XLA Ops:
  6.5 4.9 %stack.2 = bf16[16,216,1152]{2,1,0:T(8,128)(2,1)} broadcast(bf16[216,1152]{1,0:T(8,128)(2,1)} %param.11), dimensions={1,2} | broadcast | bytes 8460288 | tf_op jit(solution)/shard_map/stack | solution.py:91
  11.5 9.2 %all-to-all-start = ((bf16[16,216,1152]{2,1,0:T(8,128)(2,1)}), bf16[16,216,1152]{2,1,0:T(8,128)(2,1)}, u32[]{:S(2)}, u32[]{:S(2)}) async-start(bf16[16,216,1152]{2,1,0:T(8,128)(2,1)} %stack.2), calls=%async_computation.1 | async-start | bytes 15925248 | tf_op jit(solution)/shard_map/all_to_all | solution.py:91
  21.8 1.0 fusion.55
  22.8 64.6 %all-gather.2.cloned.1.call-done = bf16[1,1024,1152]{2,1,0:T(8,128)(2,1)} async-done(((bf16[1,128,1152]{2,1,0:T(8,128)(2,1)}), bf16[1,1024,1152]{2,1,0:T(8,128)(2,1)}) %all-gather.2.cloned.1.call-update) | async-done | bytes 2359312 | tf_op jit(solution)/shard_map/all_gather | solution.py:70
  87.4 3.3 fusion.39
  90.7 0.9 slice_bitcast_fusion.6
  92.5 16.3 %while.10 = (s32[]{:T(128)}, bf16[2,1,512,2,72]{2,4,3,1,0:T(8,128)(2,1)}, bf16[2,1,512,2,72]{2,4,3,1,0:T(8,128)(2,1)}, bf16[1,1024,2,72]{1,3,2,0:T(8,128)(2,1)}, bf16[1,1024,2,72]{1,3,2,0:T(8,128)(2,1)}, /*index=5*/s32[]{:T(128)}) while((s32[]{:T(128)}, bf16[2,1,512,2,72]{2,4,3,1,0:T(8,128)(2,1)}, bf16[2,1,512,2,72]{2,4,3,1,0:T(8,128)(2,1)}, ...), condition=%wide.region_5.6_spmd, body=%wide.region_2.5_spmd.sunk | while | flops 307307520 | bytes 9281621 | solution.py:45
  92.5 4.5 %fusion.91 = (f32[2,512]{1,0:T(2,128)S(1)}, f32[2,512,1024]{2,1,0:T(8,128)}) fusion(bf16[1,1024,2,72]{1,3,2,0:T(8,128)(2,1)} %get-tuple-element.118, bf16[2,1,512,2,72]{2,4,3,1,0:T(8,128)(2,1)} %get-tuple-element.117, s32[]{:T(128)S(6)} %copy.37), kind=kOutput, calls=%fused_computation.80.clone.1 | convolution fusion | flops 154141696 | bytes 4640772 | tf_op jit(solution)/shard_map/while/body/eval_jaxpr/sub | solution.py:20
  97.0 3.7 %fusion.92 = bf16[2,1,512,2,72]{2,4,3,1,0:T(8,128)(2,1)} fusion(bf16[2,1,512,2,72]{2,4,3,1,0:T(8,128)(2,1)} %get-tuple-element.110, s32[]{:T(128)S(6)} %copy.37, f32[2,512,1024]{2,1,0:T(8,128)} %get-tuple-element.101, f32[2,512]{1,0:T(2,128)S(1)} %get-tuple-element.102, bf16[1,1024,2,72]{1,3,2,0:T(8,128)(2,1)} %get-tuple-element.119), kind=kOutput, calls=%fused_computation.9.clone.1 | convolution fusion | flops 153165824 | bytes 4640772 | tf_op jit(solution)/shard_map/while/body/eval_jaxpr/fhqk,fkhe->fqhe/dot_general | solution.py:30
  100.7 4.4 %fusion.91 = (f32[2,512]{1,0:T(2,128)S(1)}, f32[2,512,1024]{2,1,0:T(8,128)}) fusion(bf16[1,1024,2,72]{1,3,2,0:T(8,128)(2,1)} %get-tuple-element.118, bf16[2,1,512,2,72]{2,4,3,1,0:T(8,128)(2,1)} %get-tuple-element.117, s32[]{:T(128)S(6)} %copy.37), kind=kOutput, calls=%fused_computation.80.clone.1 | convolution fusion | flops 154141696 | bytes 4640772 | tf_op jit(solution)/shard_map/while/body/eval_jaxpr/sub | solution.py:20
  105.1 3.7 %fusion.92 = bf16[2,1,512,2,72]{2,4,3,1,0:T(8,128)(2,1)} fusion(bf16[2,1,512,2,72]{2,4,3,1,0:T(8,128)(2,1)} %get-tuple-element.110, s32[]{:T(128)S(6)} %copy.37, f32[2,512,1024]{2,1,0:T(8,128)} %get-tuple-element.101, f32[2,512]{1,0:T(2,128)S(1)} %get-tuple-element.102, bf16[1,1024,2,72]{1,3,2,0:T(8,128)(2,1)} %get-tuple-element.119), kind=kOutput, calls=%fused_computation.9.clone.1 | convolution fusion | flops 153165824 | bytes 4640772 | tf_op jit(solution)/shard_map/while/body/eval_jaxpr/fhqk,fkhe->fqhe/dot_general | solution.py:30
  108.8 1.3 copy.23
  110.2 2.3 convolution_convert_fusion.1
  112.5 181.4 %reduce-scatter.2.cloned.1.call-done = bf16[128,1152]{1,0:T(8,128)(2,1)} async-done(((bf16[1024,1152]{1,0:T(8,128)(2,1)}), bf16[128,1152]{1,0:T(8,128)(2,1)}) %reduce-scatter.2.cloned.1.call-update) | async-done | bytes 294928 | tf_op jit(solution)/shard_map/reduce_scatter | solution.py:78
  293.9 1.2 convert_reduce_fusion
  295.4 6.8 %convolution_convert_fusion = bf16[128,3456]{1,0:T(8,128)(2,1)} fusion(bf16[3456,1152]{1,0:T(8,128)(2,1)} %bitcast.13, bf16[1,128,1152]{2,1,0:T(8,128)(2,1)S(1)} %get-tuple-element.60, f32[1152]{0:T(1024)S(1)} %get-tuple-element.47, f32[1152]{0:T(1024)S(1)} %copy-done.3, f32[128]{0:T(128)S(1)} %add_rsqrt_fusion, f32[128]{0:T(128)S(1)} %broadcast_multiply_fusion), kind=kOutput, calls=%fused_computation.23 | convolution fusion | flops 1020542976 | bytes 9152512 | tf_op jit(solution)/shard_map/dot_general | solution.py:88
  302.1 2.2 copy.24
  304.3 28.9 %all_to_all.38 = bf16[1,128,16,216]{1,3,0,2:T(8,128)(2,1)} all-to-all(bf16[1,128,16,216]{1,3,0,2:T(8,128)(2,1)} %bitcast.129), channel_id=1, replica_groups=mesh['batch'=4,'tm'=16,'space'=8] {'tm'}, dimensions={2} | all-to-all | bytes 1769472 | tf_op jit(solution)/shard_map/all_to_all | solution.py:99
  333.2 2.7 copy.26
  335.9 3.2 fusion.76
  339.0 2.7 fusion.43
  341.7 1.5 copy.28
  343.1 13.6 %all_to_all.39 = bf16[16,128,72]{1,2,0:T(8,128)(2,1)S(1)} all-to-all(bf16[16,128,72]{1,2,0:T(8,128)(2,1)S(1)} %copy.28), channel_id=1, replica_groups=mesh['batch'=4,'tm'=16,'space'=8] {'tm'}, dimensions={0} | all-to-all | bytes 589824 | tf_op jit(solution)/shard_map/all_to_all | solution.py:103
  356.8 1.3 fusion.35
  (29 shorter events, 2.4 us)
Async XLA Ops:
  6.5 350.2 %copy-start = (bf16[1152,1152]{1,0:T(8,128)(2,1)S(1)}, bf16[1152,1152]{1,0:T(8,128)(2,1)}, u32[]{:S(2)}) copy-start(bf16[1152,1152]{1,0:T(8,128)(2,1)} %param.12) | copy-start | bytes 7962628
  11.5 9.3 %copy-start.5 = (f32[2,3,1152]{2,0,1:T(2,128)S(1)}, f32[2,3,1152]{2,0,1:T(2,128)}, u32[]{:S(2)}) copy-start(f32[2,3,1152]{2,0,1:T(2,128)} %param.13) | copy-start | bytes 82948
  11.5 9.9 %copy-start.1 = (bf16[1,128,1152]{2,1,0:T(8,128)(2,1)S(1)}, bf16[1,128,1152]{2,1,0:T(8,128)(2,1)}, u32[]{:S(2)}) copy-start(bf16[1,128,1152]{2,1,0:T(8,128)(2,1)} %param.8) | copy-start | bytes 884740
  11.5 283.9 %all-to-all-start = ((bf16[16,216,1152]{2,1,0:T(8,128)(2,1)}), bf16[16,216,1152]{2,1,0:T(8,128)(2,1)}, u32[]{:S(2)}, u32[]{:S(2)}) async-start(bf16[16,216,1152]{2,1,0:T(8,128)(2,1)} %stack.2), calls=%async_computation.1 | async-start | bytes 15925248 | tf_op jit(solution)/shard_map/all_to_all | solution.py:91
  20.7 66.7 %all-gather.2.cloned.1.call-start = ((), (), s32[]{:S(2)}) async-start(), calls=%async_computation.4 | async-start | bytes 2654208 | tf_op jit(solution)/shard_map/all_gather | solution.py:70
  22.8 271.2 %reduce-scatter.2.cloned.1.call-start = ((), (), s32[]{:S(2)}) async-start(), calls=%async_computation.5 | async-start | bytes 2654208 | tf_op jit(solution)/shard_map/reduce_scatter | solution.py:78
  92.5 17.7 %copy-start.2 = (bf16[144,1152]{1,0:T(8,128)(2,1)S(1)}, bf16[144,1152]{1,0:T(8,128)(2,1)}, u32[]{:S(2)}) copy-start(bf16[144,1152]{1,0:T(8,128)(2,1)} %param.10) | copy-start | bytes 995332
  108.8 185.1 %copy-start.4 = (f32[1152]{0:T(1024)S(1)}, f32[1152]{0:T(1024)}, u32[]{:S(2)}) copy-start(f32[1152]{0:T(1024)} %get-tuple-element.46) | copy-start | bytes 13828
  108.8 186.5 %copy-start.3 = (f32[1152]{0:T(1024)S(1)}, f32[1152]{0:T(1024)}, u32[]{:S(2)}) copy-start(f32[1152]{0:T(1024)} %get-tuple-element.48) | copy-start | bytes 13828
Sparse Core Ops, SparseCore 0:
  23.6 63.7 all-gather.1
  112.6 181.2 reduce-scatter.1
